TPU v7x, 32 devices: a whole 2x2x4 slice. The times are simulated.
32 devices in a mesh: seq: 16 (over z, y, x), doc: 2 (over core).
Axes of the slice: x: 2, y: 2, z: 4, core: 2. Of those that a mesh axis runs over, the one named last changes fastest.
Arguments:
- conv_input: bfloat16 [4096, 4352], P(('doc', 'seq')), parts along dimension 0, may hold values from -6 to 6
- gate_input: bfloat16 [4096, 4096], P(('doc', 'seq')), parts along dimension 0, may hold values from -6 to 6
- step_input: bfloat16 [4096, 64], P(('doc', 'seq')), parts along dimension 0, may hold values from -1.1 to 2.9
- conv_weight: float32 [4, 4352], replicated, may hold values from -3 to 3
- convolution_bias: float32 [4352], replicated, may hold values from -0.5 to 0.5
- step_bias: float32 [64], replicated, may hold values from -12 to -2, as said below
- decay_log: float32 [64], replicated, may hold values from -3.3 to -1, as said below
- skip_gain: float32 [64], replicated, may hold values from 0.5 to 2
- norm_gain: float32 [4096], replicated, may hold values from 0.5 to 1.5
Outputs:
- normed: bfloat16 [4096, 4096], P(('doc', 'seq')), parts along dimension 0
There are 2 independent parts, one for each index of `doc`. A program takes and returns all parts, laid end to end along the dimension named above; an argument that names none is the same for every part. Nothing has to cross between parts.
Inputs may be any that keep to these rules, and one draw needn't show every extreme that they name: `decay_log`: one value a head. `step_bias`: one value a head.
All inputs are finite; a program needn't handle non-finite values.
Results may differ from a plain program's by a relative error of at most 0.0051.
Values may be sent and summed in bfloat16 or wider, within the bound.
A program may use at most 64 MiB of HBM per device.

v0:
```python
import jax
import jax.numpy as jnp
from jax import lax
from jax.sharding import PartitionSpec as P

HEADDIM = 64
STATE = 128
HEADS = 64
STRETCH = 256


def shifted(value, axis, steps):
    count = lax.axis_size(axis)
    initial, last = (max(0, -steps), min(count, count - steps))
    return lax.ppermute(value, axis, [(source, source + steps) for source in range(initial, last)])


def gated_norm(mixed_out, gate_input, norm_gain):
    gated = mixed_out.astype(jnp.float32) * jax.nn.silu(gate_input.astype(jnp.float32))
    spread = jnp.mean(gated * gated, axis=-1, keepdims=True)
    return (gated * lax.rsqrt(spread + 1e-05) * norm_gain[None, :]).astype(jnp.bfloat16)


def convolve(conv_input, conv_weight, convolution_bias):
    tap_count = conv_weight.shape[0]
    row_count = conv_input.shape[0]
    earlier = shifted(conv_input[row_count - (tap_count - 1) :], "seq", 1)
    padded = jnp.concatenate([earlier, conv_input], axis=0).astype(jnp.float32)
    mixed = convolution_bias[None, :]
    for offset in range(tap_count):
        mixed = mixed + conv_weight[offset][None, :] * padded[offset : offset + row_count]
    return jax.nn.silu(mixed).astype(jnp.bfloat16)


def dual_form(values, step_size, decay_rate, b_rows, c_rows, block_len):
    highest = lax.Precision.HIGHEST
    row_count, head_count, head_width = values.shape
    state_width = b_rows.shape[1]
    blocks = row_count // block_len
    block_values = values.reshape(blocks, block_len, head_count, head_width)
    block_step_sizes = step_size.reshape(blocks, block_len, head_count)
    block_b = b_rows.reshape(blocks, block_len, state_width)
    block_c = c_rows.reshape(blocks, block_len, state_width)
    within = jnp.cumsum(block_step_sizes * decay_rate[None, None, :], axis=1)
    ends = within[:, -1, :]
    totals = jnp.cumsum(ends, axis=0)
    before = totals - ends
    lower = jnp.arange(block_len)[:, None] >= jnp.arange(block_len)[None, :]
    turned = jnp.transpose(within, (0, 2, 1))
    diffs = jnp.where(lower[None, None], turned[:, :, :, None] - turned[:, :, None, :], -jnp.inf)
    scores = jnp.einsum("ctn,csn->cts", block_c, block_b, precision=highest)
    mixing = (
        jnp.exp(diffs) * scores[:, None] * jnp.transpose(block_step_sizes, (0, 2, 1))[:, :, None, :]
    )
    inside = jnp.einsum("chts,cshp->cthp", mixing, block_values, precision=highest)
    tail = jnp.exp(ends[:, None, :] - within) * block_step_sizes
    weighted = tail[:, :, :, None] * block_values
    states = jnp.einsum("cshp,csn->chpn", weighted, block_b, precision=highest)
    order = jnp.arange(blocks)
    earlier_mask = order[:, None] > order[None, :]
    gap = jnp.where(earlier_mask[None], before.T[:, :, None] - totals.T[:, None, :], -jnp.inf)
    entering = jnp.einsum("hcd,dhpn->chpn", jnp.exp(gap), states, precision=highest)
    outside = jnp.exp(within)[:, :, :, None] * jnp.einsum(
        "ctn,chpn->cthp", block_c, entering, precision=highest
    )
    result = (inside + outside).reshape(row_count, head_count, head_width)
    last = totals[-1]
    final = jnp.einsum("dh,dhpn->hpn", jnp.exp(last[None, :] - totals), states, precision=highest)
    decay_sum = (before[:, None, :] + within).reshape(row_count, head_count)
    return (result, final, decay_sum, last)


def shards(
    conv_input,
    gate_input,
    step_input,
    conv_weight,
    convolution_bias,
    step_bias,
    decay_log,
    skip_gain,
    norm_gain,
):
    inner_width = HEADS * HEADDIM
    decay_rate = -jnp.exp(decay_log)
    activated = convolve(conv_input, conv_weight, convolution_bias)
    head_values, head_steps = (
        lax.all_to_all(activated[:, :inner_width], "seq", split_axis=1, concat_axis=0, tiled=True),
        lax.all_to_all(step_input, "seq", split_axis=1, concat_axis=0, tiled=True),
    )
    shared = lax.all_gather(activated[:, inner_width:], "seq", axis=0, tiled=True)
    full_rows = shared.shape[0]
    own_heads = head_steps.shape[1]
    first_head = lax.axis_index("seq") * own_heads
    own_bias = lax.dynamic_slice_in_dim(step_bias, first_head, own_heads)
    own_rate = lax.dynamic_slice_in_dim(decay_rate, first_head, own_heads)
    own_skip = lax.dynamic_slice_in_dim(skip_gain, first_head, own_heads)
    values = head_values.astype(jnp.float32).reshape(full_rows, own_heads, HEADDIM)
    shared_rows = shared.astype(jnp.float32)
    step_size = jax.nn.softplus(head_steps.astype(jnp.float32) + own_bias[None, :])
    result, final, decay_sum, last = dual_form(
        values,
        step_size,
        own_rate,
        shared_rows[:, :STATE],
        shared_rows[:, STATE:],
        min(STRETCH, full_rows),
    )
    result = result + own_skip[None, :, None] * values
    head_output = result.astype(jnp.bfloat16).reshape(full_rows, own_heads * HEADDIM)
    mixed_out = lax.all_to_all(head_output, "seq", split_axis=0, concat_axis=1, tiled=True)
    return gated_norm(mixed_out, gate_input, norm_gain)


def solution(mesh):
    in_specs = (
        P(("doc", "seq"), None),
        P(("doc", "seq"), None),
        P(("doc", "seq"), None),
        P(),
        P(),
        P(),
        P(),
        P(),
        P(),
    )
    out_specs = P(("doc", "seq"), None)
    return jax.shard_map(shards, mesh=mesh, in_specs=in_specs, out_specs=out_specs, check_vma=False)
```

profile of v0, /device:TPU:0, one launch (start us, length us, event | category | flops | bytes accessed | tf_op | source)
XLA Modules:
  0.0 146.6 jit_solution(9924083408817625690)
XLA Ops:
  6.5 0.0 copy-start.3
  6.5 8.4 %all-to-all-start.1 = ((bf16[128,16,4]{0,2,1:T(4,128)(2,1)}), bf16[128,16,4]{0,2,1:T(4,128)(2,1)S(1)}, u32[]{:S(2)}, u32[]{:S(2)}) async-start(bf16[128,16,4]{0,2,1:T(4,128)(2,1)} %bitcast.77), calls=%async_computation.1 | async-start | bytes 32768 | tf_op jit(solution)/shard_map/all_to_all | solution.py:89
  15.0 0.0 all-gather.2.cloned.1.call-start
  15.0 0.9 slice.49
  15.9 3.8 %collective-permute-start = (bf16[3,4352]{1,0:T(4,128)(2,1)S(1)}, bf16[3,4352]{1,0:T(4,128)(2,1)S(1)}, u32[]{:S(2)}, u32[]{:S(2)}) collective-permute-start(bf16[3,4352]{1,0:T(4,128)(2,1)S(1)} %slice.49), channel_id=1, source_target_pairs={{0,2},{2,4},{4,6},{6,8},{8,10},{10,12},{12,14},{14,16},{16,18},{18... | collective-permute-start | bytes 78344 | tf_op jit(solution)/shard_map/ppermute | solution.py:15
  19.8 1.2 slice_reduce_fusion.4
  21.0 1.7 %copy.46 = bf16[128,4352]{0,1:T(8,128)(2,1)S(1)} copy(bf16[128,4352]{1,0:T(8,128)(2,1)} %param.9) | data formatting | bytes 2228224 | tf_op args[0]
  22.7 0.0 copy-done.3
  22.7 0.1 dynamic_slice.9
  22.8 0.0 collective-permute-done
  22.8 0.5 copy.45
  23.3 0.0 copy-start.1
  23.3 0.8 maximum_convert_fusion
  24.2 0.0 copy-done.1
  24.2 5.5 %multiply_convert_fusion = bf16[128,4352]{0,1:T(8,128)(2,1)S(1)} fusion(f32[131,4352]{0,1:T(8,128)S(1)} %maximum_convert_fusion, f32[4352]{0:T(1024)S(1)} %get-tuple-element.7, f32[4352]{0:T(1024)S(1)} %get-tuple-element.8, f32[4352]{0:T(1024)S(1)} %get-tuple-element.6, f32[4352]{0:T(1024)S(1)} %get-tuple-element.5, f32[4352]{0:T(1024)S(1)} %copy-done.1), kind=kLoop, calls=%fused_computation.23 | loop fusion | flops 7241728 | bytes 10114048 | tf_op jit(solution)/shard_map/convert_element_type | solution.py:32
  29.7 0.0 copy-start.4
  29.7 0.0 copy-start.5
  29.7 1.0 slice.68
  30.8 0.6 slice.71
  31.4 0.0 all-gather.2.cloned.1.call-update
  31.4 0.0 all-to-all-done.1
  31.4 5.9 %all-to-all-start = ((bf16[128,16,256]{0,2,1:T(8,128)(2,1)}), bf16[128,16,256]{0,2,1:T(8,128)(2,1)S(1)}, u32[]{:S(2)}, u32[]{:S(2)}) async-start(bf16[128,16,256]{0,2,1:T(8,128)(2,1)} %bitcast), calls=%async_computation | async-start | bytes 2097152 | tf_op jit(solution)/shard_map/all_to_all | solution.py:88
  37.3 0.0 copy-done.4
  37.3 0.1 dynamic_slice.10
  37.4 0.0 copy-done.5
  37.4 0.1 dynamic_slice.11
  37.5 0.1 mul.155
  37.6 0.1 mul.156
  37.7 0.1 multiply_bitcast_fusion
  37.8 2.3 %reduce-window.6 = f32[8,4,2,128]{3,0,1,2:T(8,128)S(1)} reduce-window(f32[8,4,2,128]{3,0,1,2:T(8,128)S(1)} %copy.49, f32[]{:T(128)} %constant.30.clone.1), window={size=1x1x1x128 pad=0_0x0_0x0_0x127_0}, to_apply=%region_0.1 | reduce-window | flops 1040384 | bytes 65540 | tf_op jit(solution)/shard_map/reduce-window
  40.1 0.2 slice_reduce_fusion
  40.3 0.1 copy_bitcast_fusion
  40.4 0.2 slice_reduce_fusion.5
  40.5 0.2 reduce_window_sum.36
  40.7 0.1 fusion.40
  40.9 21.0 %all-to-all-done = bf16[128,16,256]{0,2,1:T(8,128)(2,1)S(1)} async-done(((bf16[128,16,256]{0,2,1:T(8,128)(2,1)}), bf16[128,16,256]{0,2,1:T(8,128)(2,1)S(1)}, u32[]{:S(2)}, u32[]{:S(2)}) %all-to-all-start) | async-done | bytes 1048608 | tf_op jit(solution)/shard_map/all_to_all | solution.py:88
  61.9 0.7 copy.47
  62.6 0.6 reshape_reshape.3
  63.2 24.1 %all-gather.2.cloned.1.call-done = bf16[2048,256]{0,1:T(8,128)(2,1)} async-done(((bf16[128,256]{0,1:T(8,128)(2,1)}), bf16[2048,256]{0,1:T(8,128)(2,1)}) %all-gather.2.cloned.1.call-update) | async-done | bytes 1048592 | tf_op jit(solution)/shard_map/all_gather | solution.py:91
  87.2 2.1 %fusion.41 = (bf16[2048,128]{0,1:T(8,128)(2,1)S(1)}, bf16[2048,128]{0,1:T(8,128)(2,1)}) fusion(bf16[2048,256]{0,1:T(8,128)(2,1)} %all-gather.2.cloned.1.call-done), kind=kLoop, calls=%fused_computation.71 | loop fusion | bytes 2097152 | tf_op jit(solution)/shard_map/slice | solution.py:105
  89.3 0.3 copy.54
  89.6 1.3 copy.53
  90.9 0.2 convert_multiply_fusion.1
  91.1 1.6 %fusion.21 = f32[8,4,64,128]{3,2,1,0:T(8,128)S(1)} fusion(bf16[8,256,128,1]{2,1,3,0:T(8,128)(2,1)S(1)} %bitcast.72, f32[8,256,4,64]{1,0,3,2:T(8,128)S(1)} %convert_multiply_fusion.1), kind=kOutput, calls=%fused_computation.31 | convolution fusion | flops 805306368 | bytes 3670016 | tf_op jit(solution)/shard_map/cshp,csn->chpn/dot_general | solution.py:58
  92.8 1.6 %convolution_bitcast_fusion = f32[8,4,64,128]{3,0,2,1:T(8,128)S(1)} fusion(f32[8,4,64,128]{3,2,1,0:T(8,128)S(1)} %fusion.21, f32[4,8]{1,0:T(4,128)S(1)} %bitcast.76, f32[4,8]{1,0:T(4,128)S(1)} %subtract_bitcast_fusion, pred[8,8]{1,0:T(8,128)(4,1)S(1)} %iota_compare_fusion.1), kind=kOutput, calls=%fused_computation.36 | convolution fusion | flops 25166336 | bytes 2097472 | tf_op jit(solution)/shard_map/hcd,dhpn->chpn/dot_general | solution.py:62
  94.4 1.0 fusion.25
  95.4 0.4 fusion.43
  95.8 6.2 %bitcast_add_fusion = f32[8,256,4,64]{1,3,2,0:T(8,128)S(1)} fusion(f32[8,256,4,64]{1,3,2,0:T(8,128)S(1)} %fusion.25, f32[8,4,256]{2,1,0:T(4,128)S(1)} %copy.55, f32[8,256,256]{2,1,0:T(8,128)S(1)} %fusion.43, f32[8,4,256]{2,1,0:T(4,128)S(1)} %copy.51, pred[256,256]{1,0:T(8,128)(4,1)S(1)} %iota_compare_fusion, ...), kind=kOutput, calls=%fused_computation.28 | convolution fusion | flops 1620049920 | bytes 7503872 | tf_op jit(solution)/shard_map/chts,cshp->cthp/dot_general | solution.py:55
  102.0 2.8 %copy.61 = f32[8,256,4,64]{1,0,3,2:T(8,128)} copy(f32[8,256,4,64]{1,3,2,0:T(8,128)S(1)} %bitcast_add_fusion) | data formatting | bytes 4194304 | tf_op jit(solution)/shard_map/add | solution.py:66
  104.8 1.6 %reshape.121 = f32[16,128,256]{1,0,2:T(8,128)S(1)} reshape(f32[8,256,4,64]{1,0,3,2:T(8,128)} %copy.61) | data formatting | bytes 4194304 | tf_op jit(solution)/shard_map/reshape | solution.py:66
  106.4 1.7 %fusion.20 = bf16[16,128,256]{1,2,0:T(8,128)(2,1)} fusion(f32[16,128,256]{1,0,2:T(8,128)S(1)} %reshape.121, f32[256]{0:T(256)S(1)} %mul.156, bf16[128,16,256]{0,2,1:T(8,128)(2,1)S(1)} %all-to-all-done), kind=kLoop, calls=%fused_computation.30 | loop fusion | flops 2097152 | bytes 4195328 | tf_op jit(solution)/shard_map/convert_element_type | solution.py:110
  108.1 0.0 copy-start
  108.1 4.6 %all-to-all-start.2 = ((bf16[16,128,256]{1,2,0:T(8,128)(2,1)}), bf16[16,128,256]{1,2,0:T(8,128)(2,1)S(1)}, u32[]{:S(2)}, u32[]{:S(2)}) async-start(bf16[16,128,256]{1,2,0:T(8,128)(2,1)} %fusion.20), calls=%async_computation.2 | async-start | bytes 2097152 | tf_op jit(solution)/shard_map/all_to_all | solution.py:111
  112.7 0.0 copy-done
  112.8 0.0 copy-start.2
  112.8 0.7 copy.63
  113.4 23.4 %all-to-all-done.2 = bf16[16,128,256]{1,2,0:T(8,128)(2,1)S(1)} async-done(((bf16[16,128,256]{1,2,0:T(8,128)(2,1)}), bf16[16,128,256]{1,2,0:T(8,128)(2,1)S(1)}, u32[]{:S(2)}, u32[]{:S(2)}) %all-to-all-start.2) | async-done | bytes 1048608 | tf_op jit(solution)/shard_map/all_to_all | solution.py:111
  136.8 0.7 multiply_reduce_fusion
  137.5 0.0 copy-done.2
  137.5 0.9 multiply_convert_fusion.1
  138.4 1.3 copy.64
  (14 shorter events, 0.1 us)
Async XLA Ops:
  6.5 16.2 %copy-start.3 = (f32[64]{0:T(128)S(1)}, f32[64]{0:T(128)}, u32[]{:S(2)}) copy-start(f32[64]{0:T(128)} %param.14) | copy-start | bytes 772
  6.5 24.9 %all-to-all-start.1 = ((bf16[128,16,4]{0,2,1:T(4,128)(2,1)}), bf16[128,16,4]{0,2,1:T(4,128)(2,1)S(1)}, u32[]{:S(2)}, u32[]{:S(2)}) async-start(bf16[128,16,4]{0,2,1:T(4,128)(2,1)} %bitcast.77), calls=%async_computation.1 | async-start | bytes 32768 | tf_op jit(solution)/shard_map/all_to_all | solution.py:89
  15.0 72.3 %all-gather.2.cloned.1.call-start = ((), (), s32[]{:S(2)}) async-start(), calls=%async_computation.3 | async-start | bytes 1114112 | tf_op jit(solution)/shard_map/all_gather | solution.py:91
  15.9 6.9 %collective-permute-start = (bf16[3,4352]{1,0:T(4,128)(2,1)S(1)}, bf16[3,4352]{1,0:T(4,128)(2,1)S(1)}, u32[]{:S(2)}, u32[]{:S(2)}) collective-permute-start(bf16[3,4352]{1,0:T(4,128)(2,1)S(1)} %slice.49), channel_id=1, source_target_pairs={{0,2},{2,4},{4,6},{6,8},{8,10},{10,12},{12,14},{14,16},{16,18},{18... | collective-permute-start | bytes 78344 | tf_op jit(solution)/shard_map/ppermute | solution.py:15
  23.3 0.8 copy-start.1
  29.7 7.6 %copy-start.4 = (f32[64]{0:T(128)S(1)}, f32[64]{0:T(128)}, u32[]{:S(2)}) copy-start(f32[64]{0:T(128)} %param.15) | copy-start | bytes 772
  29.7 7.7 %copy-start.5 = (f32[64]{0:T(128)S(1)}, f32[64]{0:T(128)}, u32[]{:S(2)}) copy-start(f32[64]{0:T(128)} %param.16) | copy-start | bytes 772
  31.4 30.5 %all-to-all-start = ((bf16[128,16,256]{0,2,1:T(8,128)(2,1)}), bf16[128,16,256]{0,2,1:T(8,128)(2,1)S(1)}, u32[]{:S(2)}, u32[]{:S(2)}) async-start(bf16[128,16,256]{0,2,1:T(8,128)(2,1)} %bitcast), calls=%async_computation | async-start | bytes 2097152 | tf_op jit(solution)/shard_map/all_to_all | solution.py:88
  108.1 4.6 %copy-start = (bf16[128,4096]{1,0:T(8,128)(2,1)S(1)}, bf16[128,4096]{1,0:T(8,128)(2,1)}, u32[]{:S(2)}) copy-start(bf16[128,4096]{1,0:T(8,128)(2,1)} %param.10) | copy-start | bytes 3145732
  108.1 28.7 %all-to-all-start.2 = ((bf16[16,128,256]{1,2,0:T(8,128)(2,1)}), bf16[16,128,256]{1,2,0:T(8,128)(2,1)S(1)}, u32[]{:S(2)}, u32[]{:S(2)}) async-start(bf16[16,128,256]{1,2,0:T(8,128)(2,1)} %fusion.20), calls=%async_computation.2 | async-start | bytes 2097152 | tf_op jit(solution)/shard_map/all_to_all | solution.py:111
  112.8 24.8 %copy-start.2 = (f32[4096]{0:T(1024)S(1)}, f32[4096]{0:T(1024)}, u32[]{:S(2)}) copy-start(f32[4096]{0:T(1024)} %param.17) | copy-start | bytes 49156
Sparse Core Ops, SparseCore 0:
  31.5 55.6 all-gather.1
where the time goes:
time: 147 us
  waiting for transfers between devices  68.4 us (47%)
  starting transfers between devices  22.8 us (16%)
  local copies, waits for them, and re-layouts  18.1 us (12%)
  between operations  13.7 us (9%)
  other arithmetic  12.6 us (9%)
  matrix products  10.8 us (7%)
    all_gather x1, waiting for transfers between devices, shards(): lax.all_gather(activated[:, inner_width:], 'seq', axis=0, tiled=True)  24.1 us
    all_to_all x1, waiting for transfers between devices, shards(): lax.all_to_all(head_output, 'seq', split_axis=0, concat_axis=1, tiled=True)  23.4 us
    all_to_all x1, waiting for transfers between devices, shards(): lax.all_to_all(activated[:, :inner_width], 'seq', split_axis=1, concat_ax...  21 us
    all_to_all x1, starting transfers between devices, shards(): lax.all_to_all(step_input, 'seq', split_axis=1, concat_axis=0, tiled=True)  8.44 us
    dot_general x1, matrix products, dual_form(): jnp.einsum('chts,cshp->cthp', mixing, block_values, precision=highest)  6.18 us
    all_to_all x1, starting transfers between devices, shards(): lax.all_to_all(activated[:, :inner_width], 'seq', split_axis=1, concat_ax...  5.89 us
    convert_element_type x1, other arithmetic, convolve(): return jax.nn.silu(mixed).astype(jnp.bfloat16)  5.49 us
    all_to_all x1, starting transfers between devices, shards(): lax.all_to_all(head_output, 'seq', split_axis=0, concat_axis=1, tiled=True)  4.62 us
  transfers between devices with their start and end apart: 5, of which 3 were waited for; matrix products, arithmetic and copies ran while one was open for 12% of the time, Pallas kernels for 0%

commit v1 on v0

--- a/solution.py
+++ b/solution.py
@@ -7,6 +7,26 @@
 STATE = 128
 HEADS = 64
 STRETCH = 256
+
+
+def _move_stops_all(here_x, dimension_no, v0):
+    a_now = here_x.shape
+    front = here_x.reshape(
+        *a_now[:dimension_no], v0, a_now[dimension_no] // v0, *a_now[dimension_no + 1 :]
+    )
+    tall = jnp.moveaxis(front, dimension_no, 0)
+    return tall
+
+
+def _draft_packet(body, which_dim):
+    body = jnp.moveaxis(body, 0, which_dim)
+    found_now = body.shape
+    value_now = body.reshape(
+        *found_now[:which_dim],
+        found_now[which_dim] * found_now[which_dim + 1],
+        *found_now[which_dim + 2 :]
+    )
+    return value_now
 
 
 def shifted(value, axis, steps):
@@ -84,8 +104,20 @@
     inner_width = HEADS * HEADDIM
     decay_rate = -jnp.exp(decay_log)
     activated = convolve(conv_input, conv_weight, convolution_bias)
+
+    def follow_knots_over_axis(shard_in, comm_axis, packet, message):
+        odd, piece_now = (lax.axis_size(comm_axis), lax.axis_index(comm_axis))
+        g_now = _move_stops_all(shard_in, packet, odd)
+        inbox = [g_now[piece_now]]
+        for k in [*range(1, odd)]:
+            y = g_now[piece_now ^ k]
+            inbox.append(lax.ppermute(y, comm_axis, [(pp, pp ^ k) for pp in range(odd)]))
+        g_now = jnp.stack(inbox)[piece_now ^ jnp.arange(odd)]
+        frame_out = _draft_packet(g_now, message)
+        return frame_out
+
     head_values, head_steps = (
-        lax.all_to_all(activated[:, :inner_width], "seq", split_axis=1, concat_axis=0, tiled=True),
+        follow_knots_over_axis(activated[:, :inner_width], "seq", 1, 0),
         lax.all_to_all(step_input, "seq", split_axis=1, concat_axis=0, tiled=True),
     )
     shared = lax.all_gather(activated[:, inner_width:], "seq", axis=0, tiled=True)

time: 147 us -> 167 us (1.14)
  starting transfers between devices: 22.8 us -> 46 us
  waiting for transfers between devices: 68.4 us -> 47.3 us
  local copies, waits for them, and re-layouts: 18.1 us -> 30.2 us
  other arithmetic: 12.6 us -> 16.5 us
    ppermute x0 -> x15, starting transfers between devices: none -> 30.5 us  [follow_knots_over_axis(): lax.ppermute(y, comm_axis, [(pp, pp ^ k) for pp in range(odd)])]
    all_to_all x1 -> x0, waiting for transfers between devices: 21 us -> none  [shards(): lax.all_to_all(activated[:, :inner_width], 'seq', split_axis=1, concat_ax...]
    all_to_all x1 -> x0, starting transfers between devices: 5.89 us -> none  [shards(): lax.all_to_all(activated[:, :inner_width], 'seq', split_axis=1, concat_ax...]
    all_gather x1, waiting for transfers between devices: 24.1 us -> 18.2 us  [shards(): lax.all_gather(activated[:, inner_width:], 'seq', axis=0, tiled=True)]
    ppermute x0 -> x15, waiting for transfers between devices: none -> 5.74 us  [follow_knots_over_axis(): lax.ppermute(y, comm_axis, [(pp, pp ^ k) for pp in range(odd)])]
    reshape x1 -> x2, local copies, waits for them, and re-layouts: 1.63 us -> 7.34 us  [dual_form(): result = (inside + outside).reshape(row_count, head_count, head_width)]
    add x1 -> x0, local copies, waits for them, and re-layouts: 2.79 us -> none  [dual_form(): result = (inside + outside).reshape(row_count, head_count, head_width)]
    all_to_all x1, starting transfers between devices: 8.44 us -> 5.95 us  [shards(): lax.all_to_all(step_input, 'seq', split_axis=1, concat_axis=0, tiled=True)]
  transfers between devices with their start and end apart: 5 -> 19, of which waited for: 3 -> 5; matrix products, arithmetic and copies ran while one was open for 12% -> 13% of each run, Pallas kernels for 0% -> 0%
where the time goes in v1:
time: 167 us; the launch traced here: 166 us
  waiting for transfers between devices  47.3 us (28%)
  starting transfers between devices  46 us (28%)
  local copies, waits for them, and re-layouts  30.2 us (18%)
  other arithmetic  16.5 us (10%)
  between operations  13.9 us (8%)
  matrix products  11.9 us (7%)
    ppermute x15, starting transfers between devices, follow_knots_over_axis(): lax.ppermute(y, comm_axis, [(pp, pp ^ k) for pp in range(odd)])  30.5 us
    all_to_all x1, waiting for transfers between devices, shards(): lax.all_to_all(head_output, 'seq', split_axis=0, concat_axis=1, tiled=True)  23.4 us
    all_gather x1, waiting for transfers between devices, shards(): lax.all_gather(activated[:, inner_width:], 'seq', axis=0, tiled=True)  18.2 us
    reshape x2, local copies, waits for them, and re-layouts, dual_form(): result = (inside + outside).reshape(row_count, head_count, head_width)  7.34 us
    dot_general x1, matrix products, dual_form(): jnp.einsum('chts,cshp->cthp', mixing, block_values, precision=highest)  6.18 us
    all_to_all x1, starting transfers between devices, shards(): lax.all_to_all(step_input, 'seq', split_axis=1, concat_axis=0, tiled=True)  5.95 us
    ppermute x15, waiting for transfers between devices, follow_knots_over_axis(): lax.ppermute(y, comm_axis, [(pp, pp ^ k) for pp in range(odd)])  5.74 us
    convert_element_type x1, other arithmetic, convolve(): return jax.nn.silu(mixed).astype(jnp.bfloat16)  5.49 us
  transfers between devices with their start and end apart: 19, of which 5 were waited for; matrix products, arithmetic and copies ran while one was open for 13% of the time, Pallas kernels for 0%

profile of v1, /device:TPU:0, one launch (start us, length us, event | category | flops | bytes accessed | tf_op | source)
XLA Modules:
  0.0 165.9 jit_solution(14819329394867641315)
XLA Ops:
  6.5 0.9 slice.49
  7.5 4.8 %collective-permute-start = (bf16[3,4352]{1,0:T(4,128)(2,1)S(1)}, bf16[3,4352]{1,0:T(4,128)(2,1)S(1)}, u32[]{:S(2)}, u32[]{:S(2)}) collective-permute-start(bf16[3,4352]{1,0:T(4,128)(2,1)S(1)} %slice.49), channel_id=1, source_target_pairs={{0,2},{2,4},{4,6},{6,8},{8,10},{10,12},{12,14},{14,16},{16,18},{18... | collective-permute-start | bytes 78344 | tf_op jit(solution)/shard_map/ppermute | solution.py:35
  12.3 6.0 %all-to-all-start = ((bf16[128,16,4]{0,2,1:T(4,128)(2,1)}), bf16[128,16,4]{0,2,1:T(4,128)(2,1)S(1)}, u32[]{:S(2)}, u32[]{:S(2)}) async-start(bf16[128,16,4]{0,2,1:T(4,128)(2,1)} %bitcast.135), calls=%async_computation | async-start | bytes 32768 | tf_op jit(solution)/shard_map/all_to_all | solution.py:121
  18.4 1.2 slice_reduce_fusion.4
  19.6 0.7 exponential_negate_fusion
  20.3 1.7 %copy.65 = bf16[128,4352]{0,1:T(8,128)(2,1)S(1)} copy(bf16[128,4352]{1,0:T(8,128)(2,1)} %param.9) | data formatting | bytes 2228224 | tf_op args[0]
  22.4 0.5 copy.64
  22.9 0.8 maximum_convert_fusion
  23.8 5.5 %multiply_convert_fusion = bf16[128,4352]{0,1:T(8,128)(2,1)S(1)} fusion(f32[131,4352]{0,1:T(8,128)S(1)} %maximum_convert_fusion, f32[4352]{0:T(1024)S(1)} %get-tuple-element.7, f32[4352]{0:T(1024)S(1)} %get-tuple-element.8, f32[4352]{0:T(1024)S(1)} %get-tuple-element.6, f32[4352]{0:T(1024)S(1)} %get-tuple-element.5, f32[4352]{0:T(1024)S(1)} %copy-done.4), kind=kLoop, calls=%fused_computation.24 | loop fusion | flops 7241728 | bytes 10114048 | tf_op jit(solution)/shard_map/convert_element_type | solution.py:52
  29.4 0.3 constant_dynamic-slice_fusion
  29.7 0.1 copy.66
  29.8 0.6 slice.73
  30.6 2.0 %collective-permute-start.1 = (bf16[128,256]{1,0:T(8,128)(2,1)S(1)}, bf16[128,256]{1,0:T(8,128)(2,1)S(1)}, u32[]{:S(2)}, u32[]{:S(2)}) collective-permute-start(bf16[128,256]{1,0:T(8,128)(2,1)S(1)} %bitcast.133), channel_id=1, source_target_pairs={{0,2},{2,0},{4,6},{6,4},{8,10},{10,8},{12,14},{14,12},{16,18},{18,... | collective-permute-start | bytes 196616 | tf_op jit(solution)/shard_map/ppermute | solution.py:114
  32.7 1.5 collective-permute-start.2
  34.3 0.2 collective-permute-start.3
  34.6 2.0 %collective-permute-start.4 = (bf16[128,256]{1,0:T(8,128)(2,1)S(1)}, bf16[128,256]{1,0:T(8,128)(2,1)S(1)}, u32[]{:S(2)}, u32[]{:S(2)}) collective-permute-start(bf16[128,256]{1,0:T(8,128)(2,1)S(1)} %bitcast.130), channel_id=1, source_target_pairs={{0,8},{2,10},{4,12},{6,14},{8,0},{10,2},{12,4},{14,6},{16,24},{18,... | collective-permute-start | bytes 196616 | tf_op jit(solution)/shard_map/ppermute | solution.py:114
  36.7 1.5 collective-permute-start.5
  38.3 0.1 copy.73
  38.4 0.1 copy.74
  38.6 0.1 copy.75
  39.2 0.1 copy.81
  39.6 2.3 %reduce-window.6 = f32[8,4,2,128]{3,0,1,2:T(8,128)S(1)} reduce-window(f32[8,4,2,128]{3,0,1,2:T(8,128)S(1)} %copy.84, f32[]{:T(128)} %constant.62.clone.1), window={size=1x1x1x128 pad=0_0x0_0x0_0x127_0}, to_apply=%region_0.1 | reduce-window | flops 1040384 | bytes 65540 | tf_op jit(solution)/shard_map/reduce-window
  41.8 0.2 slice_reduce_fusion
  42.1 0.2 slice_reduce_fusion.5
  42.2 0.1 fusion.40
  42.4 0.2 reduce_window_sum.36
  42.6 2.4 %collective-permute-start.6 = (bf16[128,256]{1,0:T(8,128)(2,1)S(1)}, bf16[128,256]{1,0:T(8,128)(2,1)S(1)}, u32[]{:S(2)}, u32[]{:S(2)}) collective-permute-start(bf16[128,256]{1,0:T(8,128)(2,1)S(1)} %bitcast.128), channel_id=1, source_target_pairs={{0,12},{2,14},{4,8},{6,10},{8,4},{10,6},{12,0},{14,2},{16,28},{18,... | collective-permute-start | bytes 196616 | tf_op jit(solution)/shard_map/ppermute | solution.py:114
  45.1 0.2 collective-permute-start.7
  45.2 2.9 %collective-permute-start.8 = (bf16[128,256]{1,0:T(8,128)(2,1)S(1)}, bf16[128,256]{1,0:T(8,128)(2,1)S(1)}, u32[]{:S(2)}, u32[]{:S(2)}) collective-permute-start(bf16[128,256]{1,0:T(8,128)(2,1)S(1)} %bitcast.126), channel_id=1, source_target_pairs={{0,16},{2,18},{4,20},{6,22},{8,24},{10,26},{12,28},{14,30},{16,0},... | collective-permute-start | bytes 196616 | tf_op jit(solution)/shard_map/ppermute | solution.py:114
  48.1 1.5 collective-permute-start.9
  49.7 3.3 %collective-permute-start.10 = (bf16[128,256]{1,0:T(8,128)(2,1)S(1)}, bf16[128,256]{1,0:T(8,128)(2,1)S(1)}, u32[]{:S(2)}, u32[]{:S(2)}) collective-permute-start(bf16[128,256]{1,0:T(8,128)(2,1)S(1)} %bitcast.124), channel_id=1, source_target_pairs={{0,20},{2,22},{4,16},{6,18},{8,28},{10,30},{12,24},{14,26},{16,4},... | collective-permute-start | bytes 196616 | tf_op jit(solution)/shard_map/ppermute | solution.py:114
  53.0 0.2 collective-permute-start.11
  53.2 3.8 %collective-permute-start.12 = (bf16[128,256]{1,0:T(8,128)(2,1)S(1)}, bf16[128,256]{1,0:T(8,128)(2,1)S(1)}, u32[]{:S(2)}, u32[]{:S(2)}) collective-permute-start(bf16[128,256]{1,0:T(8,128)(2,1)S(1)} %bitcast.122), channel_id=1, source_target_pairs={{0,24},{2,26},{4,28},{6,30},{8,16},{10,18},{12,20},{14,22},{16,8},... | collective-permute-start | bytes 196616 | tf_op jit(solution)/shard_map/ppermute | solution.py:114
  57.0 1.5 collective-permute-start.13
  58.5 0.3 collective-permute-done.9
  58.8 5.0 %collective-permute-start.14 = (bf16[128,256]{1,0:T(8,128)(2,1)S(1)}, bf16[128,256]{1,0:T(8,128)(2,1)S(1)}, u32[]{:S(2)}, u32[]{:S(2)}) collective-permute-start(bf16[128,256]{1,0:T(8,128)(2,1)S(1)} %bitcast.120), channel_id=1, source_target_pairs={{0,28},{2,30},{4,24},{6,26},{8,20},{10,22},{12,16},{14,18},{16,12}... | collective-permute-start | bytes 196616 | tf_op jit(solution)/shard_map/ppermute | solution.py:114
  63.8 2.5 %collective-permute-start.15 = (bf16[128,256]{1,0:T(8,128)(2,1)S(1)}, bf16[128,256]{1,0:T(8,128)(2,1)S(1)}, u32[]{:S(2)}, u32[]{:S(2)}) collective-permute-start(bf16[128,256]{1,0:T(8,128)(2,1)S(1)} %bitcast.119), channel_id=1, source_target_pairs={{0,30},{2,28},{4,26},{6,24},{8,22},{10,20},{12,18},{14,16},{16,14}... | collective-permute-start | bytes 196616 | tf_op jit(solution)/shard_map/ppermute | solution.py:114
  66.3 0.8 collective-permute-done.11
  67.2 4.6 %collective-permute-done.15 = bf16[128,256]{1,0:T(8,128)(2,1)S(1)} collective-permute-done((bf16[128,256]{1,0:T(8,128)(2,1)S(1)}, bf16[128,256]{1,0:T(8,128)(2,1)S(1)}, u32[]{:S(2)}, u32[]{:S(2)}) %collective-permute-start.15) | collective-permute-done | bytes 65568 | tf_op jit(solution)/shard_map/ppermute | solution.py:114
  71.8 0.6 gather_fusion
  72.4 1.1 copy.82
  73.5 1.2 reshape_reshape.3
  74.7 1.4 convert_multiply_fusion.1
  76.1 18.2 %all-gather.2.cloned.1.call-done = bf16[2048,256]{0,1:T(8,128)(2,1)} async-done(((bf16[128,256]{0,1:T(8,128)(2,1)}), bf16[2048,256]{0,1:T(8,128)(2,1)}) %all-gather.2.cloned.1.call-update) | async-done | bytes 1048592 | tf_op jit(solution)/shard_map/all_gather | solution.py:123
  94.3 2.3 %fusion.41 = (bf16[2048,128]{0,1:T(8,128)(2,1)}, bf16[2048,128]{0,1:T(8,128)(2,1)}) fusion(bf16[2048,256]{0,1:T(8,128)(2,1)} %all-gather.2.cloned.1.call-done), kind=kLoop, calls=%fused_computation.107 | loop fusion | bytes 2097152 | tf_op jit(solution)/shard_map/slice | solution.py:137
  96.7 2.0 %copy.89 = bf16[2048,128]{1,0:T(8,128)(2,1)} copy(bf16[2048,128]{0,1:T(8,128)(2,1)} %get-tuple-element.25) | data formatting | bytes 1048576 | tf_op jit(solution)/shard_map/slice | solution.py:137
  98.7 2.0 %copy.88 = bf16[2048,128]{1,0:T(8,128)(2,1)} copy(bf16[2048,128]{0,1:T(8,128)(2,1)} %get-tuple-element.26) | data formatting | bytes 1048576 | tf_op jit(solution)/shard_map/slice | solution.py:138
  100.8 2.7 %fusion.20 = f32[8,4,64,128]{3,2,1,0:T(8,128)S(1)} fusion(bf16[8,256,128,1]{2,1,3,0:T(8,128)(2,1)} %bitcast.114, f32[8,256,4,64]{1,0,3,2:T(8,128)S(1)} %convert_multiply_fusion.1), kind=kOutput, calls=%fused_computation.30 | convolution fusion | flops 805306368 | bytes 3670016 | tf_op jit(solution)/shard_map/cshp,csn->chpn/dot_general | solution.py:78
  103.5 1.6 convolution_bitcast_fusion
  105.1 1.0 fusion.24
  106.1 0.4 fusion.43
  106.6 0.8 copy-done.2
  107.3 6.2 %bitcast_add_fusion = f32[8,256,4,64]{1,3,2,0:T(8,128)S(1)} fusion(f32[8,256,4,64]{1,3,2,0:T(8,128)S(1)} %fusion.24, f32[8,4,256]{2,1,0:T(4,128)S(1)} %copy.90, f32[8,256,256]{2,1,0:T(8,128)S(1)} %fusion.43, f32[8,4,256]{2,1,0:T(4,128)S(1)} %copy.86, pred[256,256]{1,0:T(8,128)(4,1)S(1)} %iota_compare_fusion, bf16[8,256,4,64]{1,0,3,2:T(8,128)(2,1)S(1)} %copy-done.2, ...), kind=kOutput, calls=%fused_computation.29 | convolution fusion | flops 1620049920 | bytes 7503872 | tf_op jit(solution)/shard_map/chts,cshp->cthp/dot_general | solution.py:75
  113.5 3.2 %copy.104 = f32[8,256,4,64]{3,2,1,0:T(4,128)} copy(f32[8,256,4,64]{1,3,2,0:T(8,128)S(1)} %bitcast_add_fusion) | data formatting | bytes 4194304 | tf_op jit(solution)/shard_map/reshape | solution.py:86
  116.7 4.2 %reshape.184 = f32[16,128,256]{2,1,0:T(8,128)S(1)} reshape(f32[8,256,4,64]{3,2,1,0:T(4,128)} %copy.104) | data formatting | bytes 4194304 | tf_op jit(solution)/shard_map/reshape | solution.py:86
  120.8 1.3 add_convert_fusion
  122.1 4.6 %all-to-all-start.1 = ((bf16[16,128,256]{2,1,0:T(8,128)(2,1)}), bf16[16,128,256]{2,1,0:T(8,128)(2,1)S(1)}, u32[]{:S(2)}, u32[]{:S(2)}) async-start(bf16[16,128,256]{2,1,0:T(8,128)(2,1)} %add_convert_fusion), calls=%async_computation.1 | async-start | bytes 2097152 | tf_op jit(solution)/shard_map/all_to_all | solution.py:143
  126.8 0.7 copy.99
  127.4 23.4 %all-to-all-done.1 = bf16[16,128,256]{2,1,0:T(8,128)(2,1)S(1)} async-done(((bf16[16,128,256]{2,1,0:T(8,128)(2,1)}), bf16[16,128,256]{2,1,0:T(8,128)(2,1)S(1)}, u32[]{:S(2)}, u32[]{:S(2)}) %all-to-all-start.1) | async-done | bytes 1048608 | tf_op jit(solution)/shard_map/all_to_all | solution.py:143
  150.8 1.6 convert_bitcast_fusion
  152.4 1.9 %copy.98 = f32[128,16,256]{0,2,1:T(8,128)S(1)} copy(f32[128,16,256]{2,0,1:T(8,128)} %convert_bitcast_fusion) | data formatting | bytes 4194304 | tf_op jit(solution)/shard_map/convert_element_type | solution.py:39
  154.3 0.7 multiply_reduce_fusion
  155.1 1.7 %multiply_convert_fusion.1 = bf16[128,4096]{0,1:T(8,128)(2,1)} fusion(f32[4096]{0:T(1024)S(1)} %copy-done.5, f32[128]{0:T(128)S(1)} %add_rsqrt_fusion, bf16[128,4096]{0,1:T(8,128)(2,1)S(1)} %copy.99, f32[128,16,256]{0,2,1:T(8,128)S(1)} %copy.98), kind=kLoop, calls=%fused_computation.33 | loop fusion | flops 4718592 | bytes 4211200 | tf_op jit(solution)/shard_map/convert_element_type | solution.py:41
  156.8 2.3 %copy.100 = bf16[128,4096]{1,0:T(8,128)(2,1)} copy(bf16[128,4096]{0,1:T(8,128)(2,1)} %multiply_convert_fusion.1) | data formatting | bytes 2097152 | tf_op jit(solution)/shard_map/convert_element_type | solution.py:41
  (81 shorter events, 2.2 us)
Async XLA Ops:
  6.5 15.5 %copy-start.6 = (f32[64]{0:T(128)S(1)}, f32[64]{0:T(128)}, u32[]{:S(2)}) copy-start(f32[64]{0:T(128)} %param.14) | copy-start | bytes 772
  6.5 15.6 %copy-start.7 = (f32[64]{0:T(128)S(1)}, f32[64]{0:T(128)}, u32[]{:S(2)}) copy-start(f32[64]{0:T(128)} %param.16) | copy-start | bytes 772
  7.5 14.9 %collective-permute-start = (bf16[3,4352]{1,0:T(4,128)(2,1)S(1)}, bf16[3,4352]{1,0:T(4,128)(2,1)S(1)}, u32[]{:S(2)}, u32[]{:S(2)}) collective-permute-start(bf16[3,4352]{1,0:T(4,128)(2,1)S(1)} %slice.49), channel_id=1, source_target_pairs={{0,2},{2,4},{4,6},{6,8},{8,10},{10,12},{12,14},{14,16},{16,18},{18... | collective-permute-start | bytes 78344 | tf_op jit(solution)/shard_map/ppermute | solution.py:35
  12.3 27.1 %all-to-all-start = ((bf16[128,16,4]{0,2,1:T(4,128)(2,1)}), bf16[128,16,4]{0,2,1:T(4,128)(2,1)S(1)}, u32[]{:S(2)}, u32[]{:S(2)}) async-start(bf16[128,16,4]{0,2,1:T(4,128)(2,1)} %bitcast.135), calls=%async_computation | async-start | bytes 32768 | tf_op jit(solution)/shard_map/all_to_all | solution.py:121
  18.3 76.0 %all-gather.2.cloned.1.call-start = ((), (), s32[]{:S(2)}) async-start(), calls=%async_computation.2 | async-start | bytes 1114112 | tf_op jit(solution)/shard_map/all_gather | solution.py:123
  22.9 0.8 copy-start.4
  30.6 12.1 %collective-permute-start.1 = (bf16[128,256]{1,0:T(8,128)(2,1)S(1)}, bf16[128,256]{1,0:T(8,128)(2,1)S(1)}, u32[]{:S(2)}, u32[]{:S(2)}) collective-permute-start(bf16[128,256]{1,0:T(8,128)(2,1)S(1)} %bitcast.133), channel_id=1, source_target_pairs={{0,2},{2,0},{4,6},{6,4},{8,10},{10,8},{12,14},{14,12},{16,18},{18,... | collective-permute-start | bytes 196616 | tf_op jit(solution)/shard_map/ppermute | solution.py:114
  32.7 12.4 %collective-permute-start.2 = (bf16[128,256]{1,0:T(8,128)(2,1)S(1)}, bf16[128,256]{1,0:T(8,128)(2,1)S(1)}, u32[]{:S(2)}, u32[]{:S(2)}) collective-permute-start(bf16[128,256]{1,0:T(8,128)(2,1)S(1)} %bitcast.132), channel_id=1, source_target_pairs={{0,4},{2,6},{4,0},{6,2},{8,12},{10,14},{12,8},{14,10},{16,20},{18,... | collective-permute-start | bytes 196616 | tf_op jit(solution)/shard_map/ppermute | solution.py:114
  34.3 10.9 %collective-permute-start.3 = (bf16[128,256]{1,0:T(8,128)(2,1)S(1)}, bf16[128,256]{1,0:T(8,128)(2,1)S(1)}, u32[]{:S(2)}, u32[]{:S(2)}) collective-permute-start(bf16[128,256]{1,0:T(8,128)(2,1)S(1)} %bitcast.131), channel_id=1, source_target_pairs={{0,6},{2,4},{4,2},{6,0},{8,14},{10,12},{12,10},{14,8},{16,22},{18,... | collective-permute-start | bytes 196616 | tf_op jit(solution)/shard_map/ppermute | solution.py:114
  34.6 13.6 %collective-permute-start.4 = (bf16[128,256]{1,0:T(8,128)(2,1)S(1)}, bf16[128,256]{1,0:T(8,128)(2,1)S(1)}, u32[]{:S(2)}, u32[]{:S(2)}) collective-permute-start(bf16[128,256]{1,0:T(8,128)(2,1)S(1)} %bitcast.130), channel_id=1, source_target_pairs={{0,8},{2,10},{4,12},{6,14},{8,0},{10,2},{12,4},{14,6},{16,24},{18,... | collective-permute-start | bytes 196616 | tf_op jit(solution)/shard_map/ppermute | solution.py:114
  36.7 13.0 %collective-permute-start.5 = (bf16[128,256]{1,0:T(8,128)(2,1)S(1)}, bf16[128,256]{1,0:T(8,128)(2,1)S(1)}, u32[]{:S(2)}, u32[]{:S(2)}) collective-permute-start(bf16[128,256]{1,0:T(8,128)(2,1)S(1)} %bitcast.129), channel_id=1, source_target_pairs={{0,10},{2,8},{4,14},{6,12},{8,2},{10,0},{12,6},{14,4},{16,26},{18,... | collective-permute-start | bytes 196616 | tf_op jit(solution)/shard_map/ppermute | solution.py:114
  42.6 10.4 %collective-permute-start.6 = (bf16[128,256]{1,0:T(8,128)(2,1)S(1)}, bf16[128,256]{1,0:T(8,128)(2,1)S(1)}, u32[]{:S(2)}, u32[]{:S(2)}) collective-permute-start(bf16[128,256]{1,0:T(8,128)(2,1)S(1)} %bitcast.128), channel_id=1, source_target_pairs={{0,12},{2,14},{4,8},{6,10},{8,4},{10,6},{12,0},{14,2},{16,28},{18,... | collective-permute-start | bytes 196616 | tf_op jit(solution)/shard_map/ppermute | solution.py:114
  45.1 8.1 %collective-permute-start.7 = (bf16[128,256]{1,0:T(8,128)(2,1)S(1)}, bf16[128,256]{1,0:T(8,128)(2,1)S(1)}, u32[]{:S(2)}, u32[]{:S(2)}) collective-permute-start(bf16[128,256]{1,0:T(8,128)(2,1)S(1)} %bitcast.127), channel_id=1, source_target_pairs={{0,14},{2,12},{4,10},{6,8},{8,6},{10,4},{12,2},{14,0},{16,30},{18,... | collective-permute-start | bytes 196616 | tf_op jit(solution)/shard_map/ppermute | solution.py:114
  45.2 11.8 %collective-permute-start.8 = (bf16[128,256]{1,0:T(8,128)(2,1)S(1)}, bf16[128,256]{1,0:T(8,128)(2,1)S(1)}, u32[]{:S(2)}, u32[]{:S(2)}) collective-permute-start(bf16[128,256]{1,0:T(8,128)(2,1)S(1)} %bitcast.126), channel_id=1, source_target_pairs={{0,16},{2,18},{4,20},{6,22},{8,24},{10,26},{12,28},{14,30},{16,0},... | collective-permute-start | bytes 196616 | tf_op jit(solution)/shard_map/ppermute | solution.py:114
  48.1 10.6 %collective-permute-start.9 = (bf16[128,256]{1,0:T(8,128)(2,1)S(1)}, bf16[128,256]{1,0:T(8,128)(2,1)S(1)}, u32[]{:S(2)}, u32[]{:S(2)}) collective-permute-start(bf16[128,256]{1,0:T(8,128)(2,1)S(1)} %bitcast.125), channel_id=1, source_target_pairs={{0,18},{2,16},{4,22},{6,20},{8,26},{10,24},{12,30},{14,28},{16,2},... | collective-permute-start | bytes 196616 | tf_op jit(solution)/shard_map/ppermute | solution.py:114
  49.7 14.2 %collective-permute-start.10 = (bf16[128,256]{1,0:T(8,128)(2,1)S(1)}, bf16[128,256]{1,0:T(8,128)(2,1)S(1)}, u32[]{:S(2)}, u32[]{:S(2)}) collective-permute-start(bf16[128,256]{1,0:T(8,128)(2,1)S(1)} %bitcast.124), channel_id=1, source_target_pairs={{0,20},{2,22},{4,16},{6,18},{8,28},{10,30},{12,24},{14,26},{16,4},... | collective-permute-start | bytes 196616 | tf_op jit(solution)/shard_map/ppermute | solution.py:114
  53.0 14.0 %collective-permute-start.11 = (bf16[128,256]{1,0:T(8,128)(2,1)S(1)}, bf16[128,256]{1,0:T(8,128)(2,1)S(1)}, u32[]{:S(2)}, u32[]{:S(2)}) collective-permute-start(bf16[128,256]{1,0:T(8,128)(2,1)S(1)} %bitcast.123), channel_id=1, source_target_pairs={{0,22},{2,20},{4,18},{6,16},{8,30},{10,28},{12,26},{14,24},{16,6},... | collective-permute-start | bytes 196616 | tf_op jit(solution)/shard_map/ppermute | solution.py:114
  53.2 13.9 %collective-permute-start.12 = (bf16[128,256]{1,0:T(8,128)(2,1)S(1)}, bf16[128,256]{1,0:T(8,128)(2,1)S(1)}, u32[]{:S(2)}, u32[]{:S(2)}) collective-permute-start(bf16[128,256]{1,0:T(8,128)(2,1)S(1)} %bitcast.122), channel_id=1, source_target_pairs={{0,24},{2,26},{4,28},{6,30},{8,16},{10,18},{12,20},{14,22},{16,8},... | collective-permute-start | bytes 196616 | tf_op jit(solution)/shard_map/ppermute | solution.py:114
  57.0 10.1 %collective-permute-start.13 = (bf16[128,256]{1,0:T(8,128)(2,1)S(1)}, bf16[128,256]{1,0:T(8,128)(2,1)S(1)}, u32[]{:S(2)}, u32[]{:S(2)}) collective-permute-start(bf16[128,256]{1,0:T(8,128)(2,1)S(1)} %bitcast.121), channel_id=1, source_target_pairs={{0,26},{2,24},{4,30},{6,28},{8,18},{10,16},{12,22},{14,20},{16,10}... | collective-permute-start | bytes 196616 | tf_op jit(solution)/shard_map/ppermute | solution.py:114
  58.8 8.4 %collective-permute-start.14 = (bf16[128,256]{1,0:T(8,128)(2,1)S(1)}, bf16[128,256]{1,0:T(8,128)(2,1)S(1)}, u32[]{:S(2)}, u32[]{:S(2)}) collective-permute-start(bf16[128,256]{1,0:T(8,128)(2,1)S(1)} %bitcast.120), channel_id=1, source_target_pairs={{0,28},{2,30},{4,24},{6,26},{8,20},{10,22},{12,16},{14,18},{16,12}... | collective-permute-start | bytes 196616 | tf_op jit(solution)/shard_map/ppermute | solution.py:114
  63.8 8.0 %collective-permute-start.15 = (bf16[128,256]{1,0:T(8,128)(2,1)S(1)}, bf16[128,256]{1,0:T(8,128)(2,1)S(1)}, u32[]{:S(2)}, u32[]{:S(2)}) collective-permute-start(bf16[128,256]{1,0:T(8,128)(2,1)S(1)} %bitcast.119), channel_id=1, source_target_pairs={{0,30},{2,28},{4,26},{6,24},{8,22},{10,20},{12,18},{14,16},{16,14}... | collective-permute-start | bytes 196616 | tf_op jit(solution)/shard_map/ppermute | solution.py:114
  100.8 4.3 %copy-start.1 = (bf16[2048,128]{1,0:T(8,128)(2,1)S(1)}, bf16[2048,128]{1,0:T(8,128)(2,1)}, u32[]{:S(2)}) copy-start(bf16[2048,128]{1,0:T(8,128)(2,1)} %copy.88) | copy-start | bytes 1572868
  105.1 1.0 copy-start
  106.1 1.2 copy-start.2
  122.1 4.6 %copy-start.3 = (bf16[128,4096]{1,0:T(8,128)(2,1)S(1)}, bf16[128,4096]{1,0:T(8,128)(2,1)}, u32[]{:S(2)}) copy-start(bf16[128,4096]{1,0:T(8,128)(2,1)} %param.10) | copy-start | bytes 3145732
  122.1 28.7 %all-to-all-start.1 = ((bf16[16,128,256]{2,1,0:T(8,128)(2,1)}), bf16[16,128,256]{2,1,0:T(8,128)(2,1)S(1)}, u32[]{:S(2)}, u32[]{:S(2)}) async-start(bf16[16,128,256]{2,1,0:T(8,128)(2,1)} %add_convert_fusion), calls=%async_computation.1 | async-start | bytes 2097152 | tf_op jit(solution)/shard_map/all_to_all | solution.py:143
  154.3 0.8 copy-start.5
Sparse Core Ops, SparseCore 0:
  39.5 54.7 all-gather.1
